TPU v7x, 32 devices: a whole 2x2x4 slice. The times are simulated.
32 devices in a mesh: groups: 2 (over y), ctx: 4 (over z), dp: 2 (over x), mp: 2 (over core).
Axes of the slice: x: 2, y: 2, z: 4, core: 2. Of those that a mesh axis runs over, the one named last changes fastest.
Arguments:
- byte_ids: int32 [4, 1024], P(('groups', 'dp'), 'ctx'), parts along dimension 0, may hold values from 0 to 255
- lengths: int32 [4], P(('groups', 'dp')), parts along dimension 0, may hold values from 128 to 1024, as said below
- hidden: bfloat16 [4, 256, 768], P(('groups', 'dp'), 'ctx'), parts along dimension 0
- w_qkv: bfloat16 [768, 3, 768], P(None, None, 'mp'), may hold values from -0.21875 to 0.21875
- w_out: bfloat16 [768, 768], P('mp'), may hold values from -0.21875 to 0.21875
- w_up: bfloat16 [4, 768, 768], P(None, None, 'mp'), may hold values from -0.109375 to 0.109375
- w_head: bfloat16 [768, 256], P('mp'), may hold values from -0.21875 to 0.21875
Outputs:
- grad_hidden: bfloat16 [4, 256, 768], P(('groups', 'dp'), 'ctx'), parts along dimension 0
There are 2 independent parts, one for each index of `groups`. A program takes and returns all parts, laid end to end along the dimension named above; an argument that names none is the same for every part. Nothing has to cross between parts.
Inputs may be any that keep to these rules, and one draw needn't show every extreme that they name: `lengths`: each document's valid byte count; in every draw some document is full, with 1024 valid bytes.
All inputs are finite; a program needn't handle non-finite values.
Results may differ from a plain program's by a relative error of at most 0.025.
Values may be sent and summed in bfloat16 or wider, within the bound.
A program may use at most 64 MiB of HBM per device.

v0:
```python
import jax
import jax.numpy as jnp
from jax import lax
from jax.sharding import PartitionSpec as P

HEAD_DIM = 64


def with_halo(x, sides, width):
    for axis, dim in sides:
        devices, length = (lax.axis_size(axis), x.shape[dim])
        up = [(i, (i + 1) % devices) for i in range(devices - 1)]
        down = [(j, i) for i, j in up]
        last = lax.slice_in_dim(x, length - width, length, axis=dim)
        initial = lax.slice_in_dim(x, 0, width, axis=dim)
        before = lax.ppermute(last, axis, up)
        after = lax.ppermute(initial, axis, down)
        x = jnp.concatenate([before, x, after], axis=dim)
    return x


def pair_sum(values):
    return lax.psum(values, "mp")


def edges(values):
    return with_halo(values, (("ctx", 0),), 1)


def gelu_grad(pre_act, incoming):
    result, pullback = jax.vjp(jax.nn.gelu, pre_act)
    return pullback(incoming)[0]


def body(byte_ids, lengths, hidden, w_qkv, w_out, w_up, w_head):
    inputs = hidden[0]
    rows = inputs.shape[0]
    model_width = inputs.shape[1]
    split_width = w_qkv.shape[2]
    own_heads = split_width // HEAD_DIM
    scaling = HEAD_DIM ** (-0.5)
    length = lengths[0]
    my_first = lax.axis_index("ctx") * rows
    byte_rows = 4 * rows
    flat_qkv = w_qkv.reshape(model_width, 3 * split_width)
    projected = jnp.dot(inputs, flat_qkv, preferred_element_type=jnp.float32).astype(jnp.bfloat16)
    projected = projected.reshape(rows, 3, own_heads, HEAD_DIM)
    queries = projected[:, 0]
    key_rows = projected[:, 1]
    value_rows = projected[:, 2]

    def usable(first_row, count):
        return 4 * (first_row + jnp.arange(count, dtype=jnp.int32)) < length

    running = jnp.full((rows, own_heads), -1e30, jnp.float32)
    key_piece = lax.all_gather(key_rows, "ctx", axis=0, tiled=True)
    value_piece = lax.all_gather(value_rows, "ctx", axis=0, tiled=True)
    keep = usable(jnp.int32(0), key_piece.shape[0])[None, None, :]
    scores = (
        jnp.einsum("qhd,khd->qhk", queries, key_piece, preferred_element_type=jnp.float32) * scaling
    )
    newest = jnp.maximum(running, jnp.max(jnp.where(keep, scores, -1e30), axis=-1))
    weights = jnp.where(keep, jnp.exp(scores - newest[..., None]), 0.0)
    totals = jnp.sum(weights, axis=-1)
    weighted = jnp.einsum(
        "qhk,khd->qhd",
        weights.astype(jnp.bfloat16),
        value_piece,
        preferred_element_type=jnp.float32,
    )
    weighted, running, totals = (weighted, newest, totals)
    attn_heads = (weighted / totals[..., None]).astype(jnp.bfloat16)
    attn = attn_heads.reshape(rows, split_width)
    log_norm = running + jnp.log(totals)
    context = (
        inputs.astype(jnp.float32)
        + pair_sum(jnp.dot(attn, w_out, preferred_element_type=jnp.float32))
    ).astype(jnp.bfloat16)
    extended = edges(context)
    tap_outputs = [
        jnp.dot(extended, w_up[tap], preferred_element_type=jnp.float32) for tap in range(4)
    ]
    phases = []
    for phase in range(4):
        phase_sum = jnp.zeros((rows, split_width), jnp.float32)
        for tap in range(4):
            shifted = 1 + (phase + tap - 1) // 4
            phase_sum = phase_sum + tap_outputs[tap][shifted : shifted + rows]
        phases.append(phase_sum)
    pre_act = jnp.stack(phases, axis=1).reshape(byte_rows, split_width)
    activated = jax.nn.gelu(pre_act).astype(jnp.bfloat16)
    logits = pair_sum(jnp.dot(activated, w_head, preferred_element_type=jnp.float32))
    byte_first = lax.axis_index("ctx") * byte_rows
    byte_mask = byte_first + jnp.arange(byte_rows, dtype=jnp.int32) < length
    inverse = 1.0 / length.astype(jnp.float32)
    softmaxed = jax.nn.softmax(logits, axis=-1)
    onehot = (byte_ids[0][:, None] == jnp.arange(logits.shape[1], dtype=jnp.int32)[None, :]).astype(
        jnp.float32
    )
    logit_grad = ((softmaxed - onehot) * jnp.where(byte_mask, inverse, 0.0)[:, None]).astype(
        jnp.bfloat16
    )
    act_grad = jnp.dot(logit_grad, w_head.T, preferred_element_type=jnp.float32)
    pre_grad = gelu_grad(pre_act, act_grad).astype(jnp.bfloat16)
    grad_ext = edges(pre_grad.reshape(rows, 4 * split_width)).reshape(byte_rows + 8, split_width)
    partial_grad = jnp.zeros((rows, model_width), jnp.float32)
    for offset in range(4):
        window = grad_ext[5 - offset : 5 - offset + byte_rows].astype(jnp.float32)
        tap_sum = jnp.sum(window.reshape(rows, 4, split_width), axis=1).astype(jnp.bfloat16)
        partial_grad = partial_grad + jnp.dot(
            tap_sum, w_up[offset].T, preferred_element_type=jnp.float32
        )
    context_grad = pair_sum(partial_grad)
    attn_grad = jnp.dot(
        context_grad.astype(jnp.bfloat16), w_out.T, preferred_element_type=jnp.float32
    ).astype(jnp.bfloat16)
    attn_grad = attn_grad.reshape(rows, own_heads, HEAD_DIM)
    row_dots = jnp.sum(attn_grad.astype(jnp.float32) * attn_heads.astype(jnp.float32), axis=-1)
    key_piece = lax.all_gather(key_rows, "ctx", axis=0, tiled=True)
    value_piece = lax.all_gather(value_rows, "ctx", axis=0, tiled=True)
    keep = usable(jnp.int32(0), key_piece.shape[0])[None, None, :]
    scores = (
        jnp.einsum("qhd,khd->qhk", queries, key_piece, preferred_element_type=jnp.float32) * scaling
    )
    probs = jnp.where(keep, jnp.exp(scores - log_norm[..., None]), 0.0)
    product = jnp.einsum("qhd,khd->qhk", attn_grad, value_piece, preferred_element_type=jnp.float32)
    score_grad = (probs * (product - row_dots[..., None])).astype(jnp.bfloat16)
    query_sum = jnp.einsum(
        "qhk,khd->qhd", score_grad, key_piece, preferred_element_type=jnp.float32
    )
    query_grad = (query_sum * scaling).astype(jnp.bfloat16)
    key_keep = usable(my_first, rows)[None, None, :]
    norm_all, dots_all = (
        lax.all_gather(log_norm, "ctx", axis=0, tiled=True),
        lax.all_gather(row_dots, "ctx", axis=0, tiled=True),
    )
    query_piece = lax.all_gather(queries, "ctx", axis=0, tiled=True)
    outgrad_piece = lax.all_gather(attn_grad, "ctx", axis=0, tiled=True)
    count = query_piece.shape[0]
    scores = (
        jnp.einsum("qhd,khd->qhk", query_piece, key_rows, preferred_element_type=jnp.float32)
        * scaling
    )
    probs = jnp.where(key_keep, jnp.exp(scores - norm_all[..., None]), 0.0)
    product = jnp.einsum(
        "qhd,khd->qhk", outgrad_piece, value_rows, preferred_element_type=jnp.float32
    )
    score_grad = (probs * (product - dots_all[..., None])).astype(jnp.bfloat16)
    key_sum = jnp.einsum(
        "qhk,qhd->khd", score_grad, query_piece, preferred_element_type=jnp.float32
    )
    value_sum = jnp.einsum(
        "qhk,qhd->khd",
        probs.astype(jnp.bfloat16),
        outgrad_piece,
        preferred_element_type=jnp.float32,
    )
    key_sum, value_sum = (key_sum, value_sum)
    key_grad = (key_sum * scaling).astype(jnp.bfloat16)
    value_grad = value_sum.astype(jnp.bfloat16)
    stacked = jnp.stack([query_grad, key_grad, value_grad], axis=1).reshape(rows, 3 * split_width)
    back_proj = pair_sum(jnp.dot(stacked, flat_qkv.T, preferred_element_type=jnp.float32))
    input_grad = (context_grad + back_proj).astype(jnp.bfloat16)
    return input_grad[None]


def solution(mesh):
    placed = (
        P(("groups", "dp"), "ctx"),
        P(("groups", "dp")),
        P(("groups", "dp"), "ctx", None),
        P(None, None, "mp"),
        P("mp", None),
        P(None, None, "mp"),
        P("mp", None),
    )
    return jax.shard_map(
        body,
        mesh=mesh,
        in_specs=placed,
        out_specs=P(("groups", "dp"), "ctx", None),
        check_vma=False,
    )
```

profile of v0, /device:TPU:0, one launch (start us, length us, event | category | flops | bytes accessed | tf_op | source)
XLA Modules:
  0.0 255.1 jit_solution(12642925866357019696)
XLA Ops:
  7.3 2.6 %copy.24 = bf16[768,3,384]{0,2,1:T(8,128)(2,1)S(1)} copy(bf16[768,3,384]{2,0,1:T(8,128)(2,1)} %param.10) | data formatting | bytes 3538944 | tf_op args[3]
  12.2 17.3 %all-gather.1 = bf16[256,1,6,64]{3,2,1,0:T(8,128)(2,1)S(1)} all-gather(bf16[64,1,6,64]{3,2,1,0:T(8,128)(2,1)S(1)} %get-tuple-element.11), channel_id=3, replica_groups=mesh['groups'=2,'ctx'=4,'dp'=2,'mp'=2] {'ctx'}, dimensions={0}, use_global_device_ids=true | all-gather | bytes 245760 | tf_op jit(solution)/shard_map/all_gather | solution.py:56
  32.7 16.3 %all-gather = bf16[256,1,6,64]{3,2,1,0:T(8,128)(2,1)S(1)} all-gather(bf16[64,1,6,64]{3,2,1,0:T(8,128)(2,1)S(1)} %get-tuple-element.9), channel_id=2, replica_groups=mesh['groups'=2,'ctx'=4,'dp'=2,'mp'=2] {'ctx'}, dimensions={0}, use_global_device_ids=true | all-gather | bytes 245760 | tf_op jit(solution)/shard_map/all_gather | solution.py:57
  52.5 18.5 %all-reduce.5.cloned.1.call-done = f32[64,768]{1,0:T(8,128)} async-done(((f32[64,768]{1,0:T(8,128)}), f32[64,768]{1,0:T(8,128)}) %all-reduce.5.cloned.1.call-update) | async-done | bytes 196624 | tf_op jit(solution)/shard_map/psum | solution.py:23
  72.0 3.6 %collective-permute-start = (bf16[1,768]{1,0:T(2,128)(2,1)S(1)}, bf16[1,768]{1,0:T(2,128)(2,1)S(1)}, u32[]{:S(2)}, u32[]{:S(2)}) collective-permute-start(bf16[1,768]{1,0:T(2,128)(2,1)S(1)} %get-tuple-element.17), channel_id=1, source_target_pairs={{0,4},{4,8},{8,12},{1,5},{5,9},{9,13},{2,6},{6,10},{10,14},{3,7},{... | collective-permute-start | bytes 4616 | tf_op jit(solution)/shard_map/ppermute | solution.py:16
  77.0 4.2 %collective-permute-done.1 = bf16[1,768]{1,0:T(2,128)(2,1)S(1)} collective-permute-done((bf16[1,768]{1,0:T(2,128)(2,1)S(1)}, bf16[1,768]{1,0:T(2,128)(2,1)S(1)}, u32[]{:S(2)}, u32[]{:S(2)}) %collective-permute-start.1) | collective-permute-done | bytes 1568 | tf_op jit(solution)/shard_map/ppermute | solution.py:17
  87.6 2.0 fusion.67
  90.2 17.8 %all-reduce.7.cloned.1.call-done = f32[256,256]{1,0:T(8,128)} async-done(((f32[256,256]{1,0:T(8,128)}), f32[256,256]{1,0:T(8,128)}) %all-reduce.7.cloned.1.call-update) | async-done | bytes 262160 | tf_op jit(solution)/shard_map/psum | solution.py:23
  110.2 1.6 fusion.45
  111.9 4.2 %collective-permute-start.2 = (bf16[1,1536]{1,0:T(2,128)(2,1)S(1)}, bf16[1,1536]{1,0:T(2,128)(2,1)}, u32[]{:S(2)}, u32[]{:S(2)}) collective-permute-start(bf16[1,1536]{1,0:T(2,128)(2,1)S(1)} %bitcast.170), channel_id=1, source_target_pairs={{0,4},{4,8},{8,12},{1,5},{5,9},{9,13},{2,6},{6,10},{10,14},{3,7},{... | collective-permute-start | bytes 9224 | tf_op jit(solution)/shard_map/ppermute | solution.py:16
  118.0 15.7 %all-gather.2 = bf16[256,1,6,64]{3,0,2,1:T(8,128)(2,1)S(1)} all-gather(bf16[64,1,6,64]{3,0,2,1:T(8,128)(2,1)S(1)} %copy.46), channel_id=4, replica_groups=mesh['groups'=2,'ctx'=4,'dp'=2,'mp'=2] {'ctx'}, dimensions={0}, use_global_device_ids=true | all-gather | bytes 245760 | tf_op jit(solution)/shard_map/all_gather | solution.py:137
  133.7 13.4 %all-gather.3 = f32[4,64,6]{1,2,0:T(8,128)S(1)} all-gather(f32[1,64,6]{1,2,0:T(8,128)S(1)} %bitcast.168), channel_id=1, replica_groups=mesh['groups'=2,'ctx'=4,'dp'=2,'mp'=2] {'ctx'}, dimensions={0}, use_global_device_ids=true | all-gather | bytes 7680 | tf_op jit(solution)/shard_map/all_gather | solution.py:134
  148.1 1.8 reduce_sum.69
  155.1 2.1 fusion.27
  162.2 2.1 convolution_add_fusion
  165.5 18.4 %all-reduce.9.cloned.1.call-done = f32[64,768]{1,0:T(8,128)} async-done(((f32[64,768]{1,0:T(8,128)}), f32[64,768]{1,0:T(8,128)}) %all-reduce.9.cloned.1.call-update) | async-done | bytes 196624 | tf_op jit(solution)/shard_map/psum | solution.py:23
  183.9 1.9 convolution_convert_fusion.2
  185.7 1.5 copy.33
  188.2 1.7 copy.37
  189.9 2.1 fusion.16
  192.0 13.4 %all-gather.4 = f32[4,64,6]{1,2,0:T(8,128)S(1)} all-gather(f32[1,64,6]{1,2,0:T(8,128)S(1)} %bitcast.169), channel_id=1, replica_groups=mesh['groups'=2,'ctx'=4,'dp'=2,'mp'=2] {'ctx'}, dimensions={0}, use_global_device_ids=true | all-gather | bytes 7680 | tf_op jit(solution)/shard_map/all_gather | solution.py:135
  205.5 17.8 %all_gather.24 = bf16[256,6,64]{2,1,0:T(8,128)(2,1)} all-gather(bf16[64,6,64]{2,1,0:T(8,128)(2,1)} %copy.37), channel_id=1, replica_groups=mesh['groups'=2,'ctx'=4,'dp'=2,'mp'=2] {'ctx'}, dimensions={0}, use_global_device_ids=true | all-gather | bytes 245760 | tf_op jit(solution)/shard_map/all_gather | solution.py:138
  228.9 18.0 %all-reduce.11.cloned.1.call-done = f32[64,768]{1,0:T(8,128)} async-done(((f32[64,768]{1,0:T(8,128)}), f32[64,768]{1,0:T(8,128)}) %all-reduce.11.cloned.1.call-update) | async-done | bytes 196624 | tf_op jit(solution)/shard_map/psum | solution.py:23
  246.9 1.7 fusion.75
  (86 shorter events, 41.1 us)
Async XLA Ops:
  6.5 44.9 %copy-start = (bf16[384,768]{1,0:T(8,128)(2,1)S(1)}, bf16[384,768]{1,0:T(8,128)(2,1)}, u32[]{:S(2)}) copy-start(bf16[384,768]{1,0:T(8,128)(2,1)} %param.11) | copy-start | bytes 1769476
  6.5 3.4 %copy-start.3 = (bf16[1,64,768]{2,1,0:T(8,128)(2,1)S(1)}, bf16[1,64,768]{2,1,0:T(8,128)(2,1)}, u32[]{:S(2)}) copy-start(bf16[1,64,768]{2,1,0:T(8,128)(2,1)} %param.9) | copy-start | bytes 294916
  6.5 64.5 %all-reduce.5.cloned.1.call-start = ((), (), s32[]{:S(2)}) async-start(), calls=%async_computation | async-start | bytes 393216 | tf_op jit(solution)/shard_map/psum | solution.py:23
  7.3 42.9 %copy-start.8 = (pred[256]{0:T(512)(128)(4,1)}, pred[256]{0:T(512)(128)(4,1)S(1)}, u32[]{:S(2)}) copy-start(pred[256]{0:T(512)(128)(4,1)S(1)} %multiply_compare_fusion) | copy-start | bytes 772
  11.6 0.7 copy-start.2
  11.6 39.8 %copy-start.1 = (bf16[64,1,6,64]{3,2,1,0:T(8,128)(2,1)}, bf16[64,1,6,64]{3,2,1,0:T(8,128)(2,1)S(1)}, u32[]{:S(2)}) copy-start(bf16[64,1,6,64]{3,2,1,0:T(8,128)(2,1)S(1)} %get-tuple-element.9) | copy-start | bytes 147460
  49.9 21.1 %copy-start.4 = (bf16[1,64,768]{2,1,0:T(8,128)(2,1)S(1)}, bf16[1,64,768]{2,1,0:T(8,128)(2,1)}, u32[]{:S(2)}) copy-start(bf16[1,64,768]{2,1,0:T(8,128)(2,1)} %param.9) | copy-start | bytes 294916
  51.4 35.0 %copy-start.5 = (bf16[64,6,64]{0,2,1:T(8,128)(2,1)}, bf16[64,6,64]{0,2,1:T(8,128)(2,1)S(1)}, u32[]{:S(2)}) copy-start(bf16[64,6,64]{0,2,1:T(8,128)(2,1)S(1)} %fusion.12) | copy-start | bytes 147460
  52.4 55.6 %all-reduce.7.cloned.1.call-start = ((), (), s32[]{:S(2)}) async-start(), calls=%async_computation.1 | async-start | bytes 524288 | tf_op jit(solution)/shard_map/psum | solution.py:23
  72.0 5.0 %collective-permute-start = (bf16[1,768]{1,0:T(2,128)(2,1)S(1)}, bf16[1,768]{1,0:T(2,128)(2,1)S(1)}, u32[]{:S(2)}, u32[]{:S(2)}) collective-permute-start(bf16[1,768]{1,0:T(2,128)(2,1)S(1)} %get-tuple-element.17), channel_id=1, source_target_pairs={{0,4},{4,8},{8,12},{1,5},{5,9},{9,13},{2,6},{6,10},{10,14},{3,7},{... | collective-permute-start | bytes 4616 | tf_op jit(solution)/shard_map/ppermute | solution.py:16
  75.6 5.5 %collective-permute-start.1 = (bf16[1,768]{1,0:T(2,128)(2,1)S(1)}, bf16[1,768]{1,0:T(2,128)(2,1)S(1)}, u32[]{:S(2)}, u32[]{:S(2)}) collective-permute-start(bf16[1,768]{1,0:T(2,128)(2,1)S(1)} %get-tuple-element.18), channel_id=1, source_target_pairs={{4,0},{8,4},{12,8},{5,1},{9,5},{13,9},{6,2},{10,6},{14,10},{7,3},{... | collective-permute-start | bytes 4616 | tf_op jit(solution)/shard_map/ppermute | solution.py:17
  86.4 23.8 %copy-start.9 = (s32[1,256]{1,0:T(1,128)S(1)}, s32[1,256]{1,0:T(1,128)}, u32[]{:S(2)}) copy-start(s32[1,256]{1,0:T(1,128)} %param.7) | copy-start | bytes 3076
  89.6 94.2 %all-reduce.9.cloned.1.call-start = ((), (), s32[]{:S(2)}) async-start(), calls=%async_computation.2 | async-start | bytes 393216 | tf_op jit(solution)/shard_map/psum | solution.py:23
  90.2 43.5 %copy-start.6 = (f32[64,6]{0,1:T(8,128)}, f32[64,6]{0,1:T(8,128)S(1)}, u32[]{:S(2)}) copy-start(f32[64,6]{0,1:T(8,128)S(1)} %log_add_fusion) | copy-start | bytes 4612
  111.9 37.9 %collective-permute-start.2 = (bf16[1,1536]{1,0:T(2,128)(2,1)S(1)}, bf16[1,1536]{1,0:T(2,128)(2,1)}, u32[]{:S(2)}, u32[]{:S(2)}) collective-permute-start(bf16[1,1536]{1,0:T(2,128)(2,1)S(1)} %bitcast.170), channel_id=1, source_target_pairs={{0,4},{4,8},{8,12},{1,5},{5,9},{9,13},{2,6},{6,10},{10,14},{3,7},{... | collective-permute-start | bytes 9224 | tf_op jit(solution)/shard_map/ppermute | solution.py:16
  116.8 33.1 %collective-permute-start.3 = (bf16[1,1536]{1,0:T(2,128)(2,1)}, bf16[1,1536]{1,0:T(2,128)(2,1)}, u32[]{:S(2)}, u32[]{:S(2)}) collective-permute-start(bf16[1,1536]{1,0:T(2,128)(2,1)} %bitcast.43), channel_id=1, source_target_pairs={{4,0},{8,4},{12,8},{5,1},{9,5},{13,9},{6,2},{10,6},{14,10},{7,3},{... | collective-permute-start | bytes 9224 | tf_op jit(solution)/shard_map/ppermute | solution.py:17
  160.7 29.2 %copy-start.7 = (f32[64,6]{0,1:T(8,128)S(1)}, f32[64,6]{0,1:T(8,128)}, u32[]{:S(2)}) copy-start(f32[64,6]{0,1:T(8,128)} %copy-done.6) | copy-start | bytes 4612
  164.2 82.7 %all-reduce.11.cloned.1.call-start = ((), (), s32[]{:S(2)}) async-start(), calls=%async_computation.3 | async-start | bytes 393216 | tf_op jit(solution)/shard_map/psum | solution.py:23
Sparse Core Ops, SparseCore 0:
  52.5 18.4 all-reduce.4
  89.8 18.2 all-reduce.6
  164.4 19.4 all-reduce.8
  229.0 17.8 all-reduce.10
where the time goes:
time: 256 us; the launch traced here: 255 us
  blocking collectives  93.9 us (37%)
  waiting for transfers between devices  77 us (30%)
  matrix products  28.3 us (11%)
  local copies, waits for them, and re-layouts  18.3 us (7%)
  between operations  14.2 us (6%)
  other arithmetic  12.9 us (5%)
  starting transfers between devices  10.6 us (4%)
    psum x4, waiting for transfers between devices, pair_sum(): return lax.psum(values, 'mp')  72.7 us
    all_gather x1, blocking collectives, body(): outgrad_piece = lax.all_gather(attn_grad, 'ctx', axis=0, tiled=True)  17.8 us
    all_gather x1, blocking collectives, body(): key_piece = lax.all_gather(key_rows, 'ctx', axis=0, tiled=True)  17.3 us
    all_gather x1, blocking collectives, body(): value_piece = lax.all_gather(value_rows, 'ctx', axis=0, tiled=True)  16.3 us
    all_gather x1, blocking collectives, body(): query_piece = lax.all_gather(queries, 'ctx', axis=0, tiled=True)  15.7 us
    all_gather x1, blocking collectives, body(): lax.all_gather(row_dots, 'ctx', axis=0, tiled=True)  13.4 us
    all_gather x1, blocking collectives, body(): lax.all_gather(log_norm, 'ctx', axis=0, tiled=True)  13.4 us
    ppermute x2, starting transfers between devices, with_halo(): before = lax.ppermute(last, axis, up)  7.88 us
  transfers between devices with their start and end apart: 8, of which 5 were waited for; matrix products, arithmetic and copies ran while one was open for 2% of the time, Pallas kernels for 0%

commit v1 on v0

--- a/solution.py
+++ b/solution.py
@@ -1,9 +1,34 @@
+import functools
 import jax
 import jax.numpy as jnp
 from jax import lax
 from jax.sharding import PartitionSpec as P
+from jax.lax import axis_index, axis_size, ppermute
 
 HEAD_DIM = 64
+
+
+def reach_things(array_here, peer_axis, dimension_no):
+    front = axis_size(peer_axis)
+    known = axis_index(peer_axis)
+    small, vec_out, high = (front, known, array_here.shape[dimension_no])
+    lower = jnp.zeros(
+        (*array_here.shape[:dimension_no], small * high, *array_here.shape[dimension_no + 1 :]),
+        array_here.dtype,
+    )
+    u_next = array_here
+    entries = [(kk, (kk + 1) % small) for kk in range(small)]
+    tick = 0
+    while tick < small:
+        tall = (vec_out - tick) % small
+        lower = lax.dynamic_update_slice_in_dim(lower, u_next, tall * high, axis=dimension_no)
+        if tick < small - 1:
+            u_next = ppermute(u_next, axis_name=peer_axis, perm=entries)
+        tick += 1
+    return lower
+
+
+form_cells = functools.partial(reach_things, peer_axis="ctx", dimension_no=0)
 
 
 def with_halo(x, sides, width):
@@ -130,10 +155,7 @@
     )
     query_grad = (query_sum * scaling).astype(jnp.bfloat16)
     key_keep = usable(my_first, rows)[None, None, :]
-    norm_all, dots_all = (
-        lax.all_gather(log_norm, "ctx", axis=0, tiled=True),
-        lax.all_gather(row_dots, "ctx", axis=0, tiled=True),
-    )
+    norm_all, dots_all = (lax.all_gather(log_norm, "ctx", axis=0, tiled=True), form_cells(row_dots))
     query_piece = lax.all_gather(queries, "ctx", axis=0, tiled=True)
     outgrad_piece = lax.all_gather(attn_grad, "ctx", axis=0, tiled=True)
     count = query_piece.shape[0]

time: 256 us -> 233 us (0.910)
  blocking collectives: 93.9 us -> 78.5 us
  waiting for transfers between devices: 77 us -> 64.6 us
  starting transfers between devices: 10.6 us -> 14.7 us
    psum x4, waiting for transfers between devices: 72.7 us -> 57.2 us  [pair_sum(): return lax.psum(values, 'mp')]
    all_gather x1 -> x0, blocking collectives: 13.4 us -> none  [body(): lax.all_gather(row_dots, 'ctx', axis=0, tiled=True)]
    ppermute x0 -> x3, starting transfers between devices: none -> 4.12 us  [reach_things(): u_next = ppermute(u_next, axis_name=peer_axis, perm=entries)]
    ppermute x0 -> x3, waiting for transfers between devices: none -> 3.26 us  [reach_things(): u_next = ppermute(u_next, axis_name=peer_axis, perm=entries)]
  transfers between devices with their start and end apart: 8 -> 11, of which waited for: 5 -> 7; matrix products, arithmetic and copies ran while one was open for 2% -> 5% of each run, Pallas kernels for 0% -> 0%
where the time goes in v1:
time: 233 us; the launch traced here: 231 us
  blocking collectives  78.5 us (34%)
  waiting for transfers between devices  64.6 us (28%)
  matrix products  28 us (12%)
  local copies, waits for them, and re-layouts  18.3 us (8%)
  starting transfers between devices  14.7 us (6%)
  between operations  14.4 us (6%)
  other arithmetic  12.8 us (5%)
    psum x4, waiting for transfers between devices, pair_sum(): return lax.psum(values, 'mp')  57.2 us
    all_gather x1, blocking collectives, body(): key_piece = lax.all_gather(key_rows, 'ctx', axis=0, tiled=True)  17.3 us
    all_gather x1, blocking collectives, body(): value_piece = lax.all_gather(value_rows, 'ctx', axis=0, tiled=True)  16.3 us
    all_gather x1, blocking collectives, body(): outgrad_piece = lax.all_gather(attn_grad, 'ctx', axis=0, tiled=True)  15.8 us
    all_gather x1, blocking collectives, body(): query_piece = lax.all_gather(queries, 'ctx', axis=0, tiled=True)  15.3 us
    all_gather x1, blocking collectives, body(): lax.all_gather(log_norm, 'ctx', axis=0, tiled=True)  13.8 us
    ppermute x2, starting transfers between devices, with_halo(): before = lax.ppermute(last, axis, up)  7.88 us
    dot_general x4, matrix products, body(): jnp.dot(tap_sum, w_up[offset].T, preferred_element_type=jnp.float32)  6.98 us
  transfers between devices with their start and end apart: 11, of which 7 were waited for; matrix products, arithmetic and copies ran while one was open for 5% of the time, Pallas kernels for 0%

profile of v1, /device:TPU:0, one launch (start us, length us, event | category | flops | bytes accessed | tf_op | source)
XLA Modules:
  0.0 231.3 jit_solution(7659285613616905063)
XLA Ops:
  7.3 2.6 %copy.24 = bf16[768,3,384]{0,2,1:T(8,128)(2,1)S(1)} copy(bf16[768,3,384]{2,0,1:T(8,128)(2,1)} %param.10) | data formatting | bytes 3538944 | tf_op args[3]
  12.2 17.3 %all-gather.1 = bf16[256,1,6,64]{3,2,1,0:T(8,128)(2,1)S(1)} all-gather(bf16[64,1,6,64]{3,2,1,0:T(8,128)(2,1)S(1)} %get-tuple-element.11), channel_id=3, replica_groups=mesh['groups'=2,'ctx'=4,'dp'=2,'mp'=2] {'ctx'}, dimensions={0}, use_global_device_ids=true | all-gather | bytes 245760 | tf_op jit(solution)/shard_map/all_gather | solution.py:81
  32.7 16.3 %all-gather = bf16[256,1,6,64]{3,2,1,0:T(8,128)(2,1)S(1)} all-gather(bf16[64,1,6,64]{3,2,1,0:T(8,128)(2,1)S(1)} %get-tuple-element.9), channel_id=2, replica_groups=mesh['groups'=2,'ctx'=4,'dp'=2,'mp'=2] {'ctx'}, dimensions={0}, use_global_device_ids=true | all-gather | bytes 245760 | tf_op jit(solution)/shard_map/all_gather | solution.py:82
  53.1 18.0 %all-reduce.5.cloned.1.call-done = f32[64,768]{1,0:T(8,128)} async-done(((f32[64,768]{1,0:T(8,128)}), f32[64,768]{1,0:T(8,128)}) %all-reduce.5.cloned.1.call-update) | async-done | bytes 196624 | tf_op jit(solution)/shard_map/psum | solution.py:48
  72.0 3.6 %collective-permute-start = (bf16[1,768]{1,0:T(2,128)(2,1)S(1)}, bf16[1,768]{1,0:T(2,128)(2,1)S(1)}, u32[]{:S(2)}, u32[]{:S(2)}) collective-permute-start(bf16[1,768]{1,0:T(2,128)(2,1)S(1)} %get-tuple-element.17), channel_id=1, source_target_pairs={{0,4},{4,8},{8,12},{1,5},{5,9},{9,13},{2,6},{6,10},{10,14},{3,7},{... | collective-permute-start | bytes 4616 | tf_op jit(solution)/shard_map/ppermute | solution.py:41
  77.0 4.1 %collective-permute-done.1 = bf16[1,768]{1,0:T(2,128)(2,1)S(1)} collective-permute-done((bf16[1,768]{1,0:T(2,128)(2,1)S(1)}, bf16[1,768]{1,0:T(2,128)(2,1)S(1)}, u32[]{:S(2)}, u32[]{:S(2)}) %collective-permute-start.1) | collective-permute-done | bytes 1568 | tf_op jit(solution)/shard_map/ppermute | solution.py:42
  87.6 2.0 fusion.64
  89.7 15.3 %all-gather.2 = bf16[256,1,6,64]{3,0,2,1:T(8,128)(2,1)S(1)} all-gather(bf16[64,1,6,64]{3,0,2,1:T(8,128)(2,1)S(1)} %copy.45), channel_id=4, replica_groups=mesh['groups'=2,'ctx'=4,'dp'=2,'mp'=2] {'ctx'}, dimensions={0}, use_global_device_ids=true | all-gather | bytes 245760 | tf_op jit(solution)/shard_map/all_gather | solution.py:159
  105.0 3.1 %all-reduce.7.cloned.1.call-done = f32[256,256]{1,0:T(8,128)} async-done(((f32[256,256]{1,0:T(8,128)}), f32[256,256]{1,0:T(8,128)}) %all-reduce.7.cloned.1.call-update) | async-done | bytes 262160 | tf_op jit(solution)/shard_map/psum | solution.py:48
  110.2 1.6 fusion.42
  111.9 4.2 %collective-permute-start.2 = (bf16[1,1536]{1,0:T(2,128)(2,1)S(1)}, bf16[1,1536]{1,0:T(2,128)(2,1)}, u32[]{:S(2)}, u32[]{:S(2)}) collective-permute-start(bf16[1,1536]{1,0:T(2,128)(2,1)S(1)} %bitcast.158), channel_id=1, source_target_pairs={{0,4},{4,8},{8,12},{1,5},{5,9},{9,13},{2,6},{6,10},{10,14},{3,7},{... | collective-permute-start | bytes 9224 | tf_op jit(solution)/shard_map/ppermute | solution.py:41
  118.1 13.8 %all-gather.3 = f32[4,64,6]{1,2,0:T(8,128)S(1)} all-gather(f32[1,64,6]{1,2,0:T(8,128)S(1)} %bitcast.157), channel_id=1, replica_groups=mesh['groups'=2,'ctx'=4,'dp'=2,'mp'=2] {'ctx'}, dimensions={0}, use_global_device_ids=true | all-gather | bytes 7680 | tf_op jit(solution)/shard_map/all_gather | solution.py:158
  132.8 1.8 reduce_sum.69
  139.8 2.1 fusion.24
  146.9 2.1 convolution_add_fusion
  150.2 18.4 %all-reduce.9.cloned.1.call-done = f32[64,768]{1,0:T(8,128)} async-done(((f32[64,768]{1,0:T(8,128)}), f32[64,768]{1,0:T(8,128)}) %all-reduce.9.cloned.1.call-update) | async-done | bytes 196624 | tf_op jit(solution)/shard_map/psum | solution.py:48
  168.6 1.9 convolution_convert_fusion.2
  170.4 1.5 copy.33
  173.0 1.8 collective-permute-start.4
  174.8 2.1 fusion.12
  179.5 15.8 %all_gather.21 = bf16[256,6,64]{2,1,0:T(8,128)(2,1)} all-gather(bf16[64,6,64]{2,1,0:T(8,128)(2,1)S(1)} %copy.37), channel_id=1, replica_groups=mesh['groups'=2,'ctx'=4,'dp'=2,'mp'=2] {'ctx'}, dimensions={0}, use_global_device_ids=true | all-gather | bytes 245760 | tf_op jit(solution)/shard_map/all_gather | solution.py:160
  199.3 2.8 %collective-permute-done.6 = f32[64,6]{0,1:T(8,128)S(1)} collective-permute-done((f32[64,6]{0,1:T(8,128)S(1)}, f32[64,6]{0,1:T(8,128)S(1)}, u32[]{:S(2)}, u32[]{:S(2)}) %collective-permute-start.6) | collective-permute-done | bytes 1568 | tf_op jit(solution)/shard_map/ppermute | solution.py:26
  205.5 17.8 %all-reduce.11.cloned.1.call-done = f32[64,768]{1,0:T(8,128)} async-done(((f32[64,768]{1,0:T(8,128)}), f32[64,768]{1,0:T(8,128)}) %all-reduce.11.cloned.1.call-update) | async-done | bytes 196624 | tf_op jit(solution)/shard_map/psum | solution.py:48
  223.2 1.6 fusion.72
  (98 shorter events, 45.4 us)
Async XLA Ops:
  6.5 44.9 %copy-start = (bf16[384,768]{1,0:T(8,128)(2,1)S(1)}, bf16[384,768]{1,0:T(8,128)(2,1)}, u32[]{:S(2)}) copy-start(bf16[384,768]{1,0:T(8,128)(2,1)} %param.11) | copy-start | bytes 1769476
  6.5 3.4 %copy-start.5 = (bf16[1,64,768]{2,1,0:T(8,128)(2,1)S(1)}, bf16[1,64,768]{2,1,0:T(8,128)(2,1)}, u32[]{:S(2)}) copy-start(bf16[1,64,768]{2,1,0:T(8,128)(2,1)} %param.9) | copy-start | bytes 294916
  6.5 64.5 %all-reduce.5.cloned.1.call-start = ((), (), s32[]{:S(2)}) async-start(), calls=%async_computation | async-start | bytes 393216 | tf_op jit(solution)/shard_map/psum | solution.py:48
  7.3 42.9 %copy-start.10 = (pred[256]{0:T(512)(128)(4,1)}, pred[256]{0:T(512)(128)(4,1)S(1)}, u32[]{:S(2)}) copy-start(pred[256]{0:T(512)(128)(4,1)S(1)} %multiply_compare_fusion) | copy-start | bytes 772
  11.6 0.7 copy-start.3
  11.6 39.8 %copy-start.1 = (bf16[64,1,6,64]{3,2,1,0:T(8,128)(2,1)}, bf16[64,1,6,64]{3,2,1,0:T(8,128)(2,1)S(1)}, u32[]{:S(2)}) copy-start(bf16[64,1,6,64]{3,2,1,0:T(8,128)(2,1)S(1)} %get-tuple-element.9) | copy-start | bytes 147460
  49.9 21.1 %copy-start.6 = (bf16[1,64,768]{2,1,0:T(8,128)(2,1)S(1)}, bf16[1,64,768]{2,1,0:T(8,128)(2,1)}, u32[]{:S(2)}) copy-start(bf16[1,64,768]{2,1,0:T(8,128)(2,1)} %param.9) | copy-start | bytes 294916
  51.4 35.0 %copy-start.7 = (bf16[64,6,64]{0,2,1:T(8,128)(2,1)}, bf16[64,6,64]{0,2,1:T(8,128)(2,1)S(1)}, u32[]{:S(2)}) copy-start(bf16[64,6,64]{0,2,1:T(8,128)(2,1)S(1)} %fusion.9) | copy-start | bytes 147460
  52.4 55.6 %all-reduce.7.cloned.1.call-start = ((), (), s32[]{:S(2)}) async-start(), calls=%async_computation.1 | async-start | bytes 524288 | tf_op jit(solution)/shard_map/psum | solution.py:48
  72.0 5.0 %collective-permute-start = (bf16[1,768]{1,0:T(2,128)(2,1)S(1)}, bf16[1,768]{1,0:T(2,128)(2,1)S(1)}, u32[]{:S(2)}, u32[]{:S(2)}) collective-permute-start(bf16[1,768]{1,0:T(2,128)(2,1)S(1)} %get-tuple-element.17), channel_id=1, source_target_pairs={{0,4},{4,8},{8,12},{1,5},{5,9},{9,13},{2,6},{6,10},{10,14},{3,7},{... | collective-permute-start | bytes 4616 | tf_op jit(solution)/shard_map/ppermute | solution.py:41
  75.6 5.5 %collective-permute-start.1 = (bf16[1,768]{1,0:T(2,128)(2,1)S(1)}, bf16[1,768]{1,0:T(2,128)(2,1)S(1)}, u32[]{:S(2)}, u32[]{:S(2)}) collective-permute-start(bf16[1,768]{1,0:T(2,128)(2,1)S(1)} %get-tuple-element.18), channel_id=1, source_target_pairs={{4,0},{8,4},{12,8},{5,1},{9,5},{13,9},{6,2},{10,6},{14,10},{7,3},{... | collective-permute-start | bytes 4616 | tf_op jit(solution)/shard_map/ppermute | solution.py:42
  86.4 23.8 %copy-start.11 = (s32[1,256]{1,0:T(1,128)S(1)}, s32[1,256]{1,0:T(1,128)}, u32[]{:S(2)}) copy-start(s32[1,256]{1,0:T(1,128)} %param.7) | copy-start | bytes 3076
  89.6 78.9 %all-reduce.9.cloned.1.call-start = ((), (), s32[]{:S(2)}) async-start(), calls=%async_computation.2 | async-start | bytes 393216 | tf_op jit(solution)/shard_map/psum | solution.py:48
  105.0 13.1 %copy-start.8 = (f32[64,6]{0,1:T(8,128)}, f32[64,6]{0,1:T(8,128)S(1)}, u32[]{:S(2)}) copy-start(f32[64,6]{0,1:T(8,128)S(1)} %log_add_fusion) | copy-start | bytes 4612
  111.9 22.7 %collective-permute-start.2 = (bf16[1,1536]{1,0:T(2,128)(2,1)S(1)}, bf16[1,1536]{1,0:T(2,128)(2,1)}, u32[]{:S(2)}, u32[]{:S(2)}) collective-permute-start(bf16[1,1536]{1,0:T(2,128)(2,1)S(1)} %bitcast.158), channel_id=1, source_target_pairs={{0,4},{4,8},{8,12},{1,5},{5,9},{9,13},{2,6},{6,10},{10,14},{3,7},{... | collective-permute-start | bytes 9224 | tf_op jit(solution)/shard_map/ppermute | solution.py:41
  116.8 17.8 %collective-permute-start.3 = (bf16[1,1536]{1,0:T(2,128)(2,1)}, bf16[1,1536]{1,0:T(2,128)(2,1)}, u32[]{:S(2)}, u32[]{:S(2)}) collective-permute-start(bf16[1,1536]{1,0:T(2,128)(2,1)} %bitcast.42), channel_id=1, source_target_pairs={{4,0},{8,4},{12,8},{5,1},{9,5},{13,9},{6,2},{10,6},{14,10},{7,3},{... | collective-permute-start | bytes 9224 | tf_op jit(solution)/shard_map/ppermute | solution.py:42
  145.5 29.3 %copy-start.9 = (f32[64,6]{0,1:T(8,128)S(1)}, f32[64,6]{0,1:T(8,128)}, u32[]{:S(2)}) copy-start(f32[64,6]{0,1:T(8,128)} %copy-done.8) | copy-start | bytes 4612
  149.0 74.3 %all-reduce.11.cloned.1.call-start = ((), (), s32[]{:S(2)}) async-start(), calls=%async_computation.3 | async-start | bytes 393216 | tf_op jit(solution)/shard_map/psum | solution.py:48
  173.0 5.5 %collective-permute-start.4 = (f32[64,6]{0,1:T(8,128)S(1)}, f32[64,6]{0,1:T(8,128)S(1)}, u32[]{:S(2)}, u32[]{:S(2)}) collective-permute-start(f32[64,6]{0,1:T(8,128)S(1)} %multiply_reduce_fusion), channel_id=1, source_target_pairs={{0,4},{4,8},{8,12},{12,0},{1,5},{5,9},{9,13},{13,1},{2,6},{6,10},{... | collective-permute-start | bytes 4616 | tf_op jit(solution)/shard_map/ppermute | solution.py:26
  176.9 25.3 %copy-start.2 = (bf16[64,1,6,64]{3,2,1,0:T(8,128)(2,1)S(1)}, bf16[64,1,6,64]{3,2,1,0:T(8,128)(2,1)}, u32[]{:S(2)}) copy-start(bf16[64,1,6,64]{3,2,1,0:T(8,128)(2,1)} %copy-done.1) | copy-start | bytes 147460
  178.4 18.1 %collective-permute-start.5 = (f32[64,6]{0,1:T(8,128)S(1)}, f32[64,6]{0,1:T(8,128)S(1)}, u32[]{:S(2)}, u32[]{:S(2)}) collective-permute-start(f32[64,6]{0,1:T(8,128)S(1)} %collective-permute-done.4), channel_id=1, source_target_pairs={{0,4},{4,8},{8,12},{12,0},{1,5},{5,9},{9,13},{13,1},{2,6},{6,10},{... | collective-permute-start | bytes 4616 | tf_op jit(solution)/shard_map/ppermute | solution.py:26
  196.6 5.5 %collective-permute-start.6 = (f32[64,6]{0,1:T(8,128)S(1)}, f32[64,6]{0,1:T(8,128)S(1)}, u32[]{:S(2)}, u32[]{:S(2)}) collective-permute-start(f32[64,6]{0,1:T(8,128)S(1)} %collective-permute-done.5), channel_id=1, source_target_pairs={{0,4},{4,8},{8,12},{12,0},{1,5},{5,9},{9,13},{13,1},{2,6},{6,10},{... | collective-permute-start | bytes 4616 | tf_op jit(solution)/shard_map/ppermute | solution.py:26
  203.2 20.0 %copy-start.4 = (f32[64,768]{1,0:T(8,128)S(1)}, f32[64,768]{1,0:T(8,128)}, u32[]{:S(2)}) copy-start(f32[64,768]{1,0:T(8,128)} %all-reduce.9.cloned.1.call-done) | copy-start | bytes 589828
Sparse Core Ops, SparseCore 0:
  52.5 18.4 all-reduce.4
  89.8 18.2 all-reduce.6
  149.1 19.4 all-reduce.8
  205.6 17.5 all-reduce.10
